TPU v7x, 32 devices: a whole 2x2x4 slice. The times are simulated.
32 devices in a mesh: pipe: 2 (over x), seq: 4 (over y, core), chan: 4 (over z).
Axes of the slice: x: 2, y: 2, z: 4, core: 2. Of those that a mesh axis runs over, the one named last changes fastest.
Arguments:
- fwd_in: bfloat16 [2, 512, 8192], P('pipe', 'seq', 'chan'), may hold values from -14 to 14
- saved_in: bfloat16 [2, 512, 8192], P('pipe', 'seq', 'chan'), may hold values from -14 to 14
- saved_conv: bfloat16 [2, 512, 8192], P('pipe', 'seq', 'chan'), may hold values from -5 to 5
- grad_out: bfloat16 [2, 512, 8192], P('pipe', 'seq', 'chan'), may hold values from -14 to 14
- filters: bfloat16 [2, 512, 8192], P('pipe', None, 'chan'), may hold values from -1.2 to 1.2
- mix_params: float32 [2, 7, 8192], P('pipe', None, 'chan'), may hold values from -1.5 to 1.5
- span_order: int32 [4], replicated, may hold values from 0 to 3, each once
Outputs:
- layer_out: bfloat16 [2, 512, 8192], P('pipe', 'seq', 'chan')
- input_grad: bfloat16 [2, 512, 8192], P('pipe', 'seq', 'chan')
- param_grad: float32 [2, 7, 8192], P('pipe', None, 'chan')
- received: bfloat16 [2, 512, 8192], P('pipe', 'seq', 'chan')
Inputs may be any that keep to these rules, and one draw needn't show every extreme that they name: span_order holds each block position once.
All inputs are finite; a program needn't handle non-finite values.
Results may differ from a plain program's by a relative error of at most 0.015.
Values may be sent and summed in bfloat16 or wider, within the bound.
A program may use at most 192 MiB of HBM per device.

v0:
```python
import math

import jax
import jax.numpy as jnp
from jax import lax
from jax.sharding import PartitionSpec as P

D = 8192


EPSILON = 1e-05


def from_partner(block, axis, apart):
    count = lax.axis_size(axis)
    route = []
    for low in range(count):
        high = low | 1 << apart
        if high != low and high < count:
            route += [(low, high), (high, low)]
    return lax.ppermute(block, axis, route)


def split_table(table):
    high_part = table.astype(jnp.bfloat16)
    low_part = (table - lax.optimization_barrier(high_part).astype(jnp.float32)).astype(
        jnp.bfloat16
    )
    return (high_part, low_part)


def table_apply(form, table_pair, data):
    high_part, low_part = table_pair
    first = jnp.einsum(form, high_part, data, preferred_element_type=jnp.float32)
    return first + jnp.einsum(form, low_part, data, preferred_element_type=jnp.float32)


def leave_apply(form, table, spectra):
    return jnp.einsum(
        form, table, spectra, preferred_element_type=jnp.float32, precision=lax.Precision.HIGH
    )


def dft_tables(block_rows):
    period = 2 * block_rows
    frequency = jnp.arange(period, dtype=jnp.int32)[:, None]
    inside = jnp.arange(block_rows, dtype=jnp.int32)[None, :]
    angle_in = 2.0 * math.pi / period * (frequency * inside % period).astype(jnp.float32)
    forward_tab = jnp.concatenate([jnp.cos(angle_in), -jnp.sin(angle_in)], axis=0)
    angle_out = (
        2.0 * math.pi / period * (frequency * (inside + block_rows) % period).astype(jnp.float32)
    )
    inverse_tab = jnp.concatenate([jnp.cos(angle_out), -jnp.sin(angle_out)], axis=0).T / period
    parity = jnp.where(frequency % 2 == 0, 1.0, -1.0).astype(jnp.float32)
    parity_rows = jnp.concatenate([parity, parity], axis=0)
    return (forward_tab, inverse_tab, parity_rows)


def spectral_product(filter_spec, data_spec, conjugate):
    half_rows = filter_spec.shape[-2] // 2
    filter_real = filter_spec[..., :half_rows, :]
    filter_imag = filter_spec[..., half_rows:, :]
    data_real = data_spec[..., :half_rows, :]
    data_imag = data_spec[..., half_rows:, :]
    if conjugate:
        real_part = filter_real * data_real + filter_imag * data_imag
        imag_part = filter_real * data_imag - filter_imag * data_real
    else:
        real_part = filter_real * data_real - filter_imag * data_imag
        imag_part = filter_real * data_imag + filter_imag * data_real
    return jnp.concatenate([real_part, imag_part], axis=-2)


def lagged_spectrum(spectra, parity_rows, distance):
    current = lax.dynamic_index_in_dim(spectra, distance, 0, keepdims=False)
    earlier = lax.dynamic_index_in_dim(spectra, jnp.maximum(distance - 1, 0), 0, keepdims=False)
    return earlier * (distance > 0).astype(jnp.float32) + parity_rows * current


def cycle_conv(signal, taps, span_order, adjoint, tables):
    forward_tab, inverse_tab, parity_rows = tables
    block_rows, slab_width = signal.shape
    spans = taps.shape[0] // block_rows
    forward_pair = split_table(forward_tab)
    spectra = table_apply("fb,dbc->dfc", forward_pair, taps.reshape(spans, block_rows, slab_width))
    own_position = span_order[lax.axis_index("seq")]
    enter_pair = split_table(inverse_tab.T) if adjoint else forward_pair
    empty = jnp.zeros((forward_tab.shape[0], slab_width), jnp.float32)
    running_sum = empty
    arrived_blocks = lax.all_gather(signal, "seq", axis=0, tiled=True).reshape(
        -1, block_rows, slab_width
    )

    def one_block(partial_value, entry_pair):
        block_values, offset = entry_pair
        source_position = span_order[offset]
        distance = source_position - own_position if adjoint else own_position - source_position

        def add_term(inner_sum):
            entering = table_apply("fb,bc->fc", enter_pair, block_values)
            return inner_sum + spectral_product(
                lagged_spectrum(spectra, parity_rows, distance), entering, adjoint
            )

        return (lax.cond(distance >= 0, add_term, lambda inner_sum: inner_sum, partial_value), None)

    offsets = jnp.arange(arrived_blocks.shape[0], dtype=jnp.int32)
    running_sum, unused = lax.scan(one_block, running_sum, (arrived_blocks, offsets))
    leave_tab = forward_tab.T if adjoint else inverse_tab
    return leave_apply("bf,fc->bc", leave_tab, running_sum).astype(jnp.bfloat16)


def long_conv(signal, taps, span_order, adjoint, tables):
    return cycle_conv(signal, taps, span_order, adjoint, tables)


def local_fields(inputs, square_sum, params):
    inv_rms = lax.rsqrt(square_sum[:, None] / D + EPSILON)
    normed = inputs * inv_rms
    scaled = normed * params[0]
    query_feat = scaled * params[1] + params[2]
    key_feat = scaled * params[3] + params[4]
    value_feat = scaled * params[5] + params[6]
    return (inv_rms, normed, scaled, query_feat, key_feat, value_feat)


def per_device(fwd_in, saved_in, saved_conv, grad_out, filters, mix_params, span_order):
    inputs = fwd_in[0].astype(jnp.float32)
    saved = saved_in[0].astype(jnp.float32)
    params = mix_params[0]
    taps = filters[0]
    tables = dft_tables(inputs.shape[0])
    forward_squares, backward_squares = lax.psum(
        (jnp.sum(inputs * inputs, axis=1), jnp.sum(saved * saved, axis=1)), "chan"
    )
    inv_rms, normed, scaled, query_feat, key_feat, value_feat = local_fields(
        inputs, forward_squares, params
    )
    mixed = (key_feat * value_feat).astype(jnp.bfloat16)
    conv = lax.optimization_barrier(long_conv(mixed, taps, span_order, False, tables))
    layer_out = (inputs + query_feat * conv.astype(jnp.float32)).astype(jnp.bfloat16)
    inv_rms, normed, scaled, query_feat, key_feat, value_feat = local_fields(
        saved, backward_squares, params
    )
    cotangent = grad_out[0].astype(jnp.float32)
    grad_conv = (cotangent * query_feat).astype(jnp.bfloat16)
    grad_mixed = lax.optimization_barrier(long_conv(grad_conv, taps, span_order, True, tables))
    grad_mixed = grad_mixed.astype(jnp.float32)
    grad_query = cotangent * saved_conv[0].astype(jnp.float32)
    grad_key = grad_mixed * value_feat
    grad_value = grad_mixed * key_feat
    grad_scaled = grad_query * params[1] + grad_key * params[3] + grad_value * params[5]
    rows = jnp.stack(
        [
            jnp.sum(grad_scaled * normed, axis=0),
            jnp.sum(grad_query * scaled, axis=0),
            jnp.sum(grad_query, axis=0),
            jnp.sum(grad_key * scaled, axis=0),
            jnp.sum(grad_key, axis=0),
            jnp.sum(grad_value * scaled, axis=0),
            jnp.sum(grad_value, axis=0),
        ]
    )
    param_grad = lax.psum(rows.astype(jnp.bfloat16), "seq").astype(jnp.float32)
    grad_normed = grad_scaled * params[0]
    cross = lax.psum(jnp.sum(grad_normed * normed, axis=1), "chan")
    input_grad = (cotangent + inv_rms * (grad_normed - normed * (cross[:, None] / D))).astype(
        jnp.bfloat16
    )
    outgoing = jnp.where(lax.axis_index("pipe") == 0, layer_out, input_grad)
    received = from_partner(outgoing, "pipe", 0)
    return (layer_out[None], input_grad[None], param_grad[None], received[None])


def solution(mesh):
    in_specs = (
        P("pipe", "seq", "chan"),
        P("pipe", "seq", "chan"),
        P("pipe", "seq", "chan"),
        P("pipe", "seq", "chan"),
        P("pipe", None, "chan"),
        P("pipe", None, "chan"),
        P(),
    )
    out_specs = (
        P("pipe", "seq", "chan"),
        P("pipe", "seq", "chan"),
        P("pipe", None, "chan"),
        P("pipe", "seq", "chan"),
    )
    return jax.shard_map(
        per_device, mesh=mesh, in_specs=in_specs, out_specs=out_specs, check_vma=False
    )
```

profile of v0, /device:TPU:0, one launch (start us, length us, event | category | flops | bytes accessed | tf_op | source)
XLA Modules:
  0.0 273.7 jit_solution(12027663556506254391)
XLA Ops:
  10.1 13.5 %psum.29 = f32[128]{0:T(128)S(1)} all-reduce(f32[128]{0:T(128)S(1)} %fusion.36), channel_id=1, replica_groups=mesh['pipe'=2,'seq'=4,'chan'=4] {'chan'}, use_global_device_ids=true, to_apply=%region_7.8 | all-reduce | flops 128 | bytes 1024 | tf_op jit(solution)/shard_map/psum | solution.py:133
  23.5 2.3 fusion.49
  29.2 2.3 fusion.63
  31.6 8.2 %add_bitcast_fusion.2 = f32[4,512,2048]{2,1,0:T(8,128)} fusion(f32[512,4,2048]{2,0,1:T(8,128)S(1)} %fusion.63, bf16[4,128,2048]{2,1,0:T(8,128)(2,1)S(1)} %bitcast.127, bf16[512,128]{1,0:T(8,128)(2,1)S(1)} %subtract_convert_fusion.1), kind=kOutput, calls=%fused_computation.26 | convolution fusion | flops 1077936128 | bytes 35782656 | tf_op jit(solution)/shard_map/fb,dbc->dfc/dot_general | solution.py:35
  39.8 7.1 %all-gather.5.cloned.1.call-done = bf16[512,2048]{1,0:T(8,128)(2,1)} async-done(((bf16[128,2048]{1,0:T(8,128)(2,1)}), bf16[512,2048]{1,0:T(8,128)(2,1)}) %all-gather.5.cloned.1.call-update) | async-done | bytes 2097168 | tf_op jit(solution)/shard_map/all_gather | solution.py:90
  46.8 2.4 broadcast.110.clone
  49.3 75.3 %while.27 = (s32[]{:T(128)}, f32[512,2048]{1,0:T(8,128)}, s32[4]{0:T(128)S(1)}, s32[4]{0:T(128)}, s32[]{:T(128)}, /*index=5*/f32[4,512,2048]{2,1,0:T(8,128)}, f3...) while((s32[]{:T(128)}, f32[512,2048]{1,0:T(8,128)}, ...), condition=%wide.region_11.12_spmd, body=%wide.region_8.11_spmd.sunk | while | flops 546308096 | bytes 51645804 | solution.py:108
  54.3 13.8 %conditional.5 = (f32[512,2048]{1,0:T(8,128)}) conditional(s32[]{:T(128)} %convert_element_type.183, f32[512,2048]{1,0:T(8,128)} %get-tuple-element.407, (s32[]{:T(128)}, f32[4,512,2048]{2,1,0:T(8,128)}, f32[512,1]{0,1:T(1,128)S(1)}, bf16[4,128,2048]{2,1,0:T(8,128)(2,1)}, s32[]{:T(128)}, /*index=5*/bf16[512,128]{1,0:T(8,128)(2,1)S(1)}, ...), branch_computations={%region_9.9_spmd, %region_10.10_spmd} | conditional | flops 546308096 | bytes 51645532 | solution.py:105
  54.4 4.0 %fusion.8 = f32[512,2048]{1,0:T(8,128)S(1)} fusion(f32[4,512,2048]{2,1,0:T(8,128)} %get-tuple-element.178, s32[]{:T(128)S(6)} %select_n.61, s32[]{:T(128)S(6)} %max.7, f32[512]{0:T(512)S(1)} %bitcast.135, f32[]{:T(128)S(6)} %convert_element_type.67), kind=kLoop, calls=%fused_computation.15 | loop fusion | flops 3145728 | bytes 12584972 | tf_op jit(solution)/shard_map/while/body/eval_jaxpr/cond/branch_1_fun/add | solution.py:77
  62.9 5.2 %maximum_add_fusion.1 = f32[512,2048]{1,0:T(8,128)} fusion(f32[512,2048]{1,0:T(8,128)} %get-tuple-element.177, f32[256,2048]{1,0:T(8,128)S(1)} %get-tuple-element.259, f32[256,2048]{1,0:T(8,128)S(1)} %get-tuple-element.258), kind=kLoop, calls=%fused_computation.13 | loop fusion | flops 2097152 | bytes 12582912 | tf_op jit(solution)/shard_map/while/body/eval_jaxpr/cond/branch_1_fun/add | solution.py:101
  73.2 13.8 %conditional.5 = (f32[512,2048]{1,0:T(8,128)}) conditional(s32[]{:T(128)} %convert_element_type.183, f32[512,2048]{1,0:T(8,128)} %get-tuple-element.407, (s32[]{:T(128)}, f32[4,512,2048]{2,1,0:T(8,128)}, f32[512,1]{0,1:T(1,128)S(1)}, bf16[4,128,2048]{2,1,0:T(8,128)(2,1)}, s32[]{:T(128)}, /*index=5*/bf16[512,128]{1,0:T(8,128)(2,1)S(1)}, ...), branch_computations={%region_9.9_spmd, %region_10.10_spmd} | conditional | flops 546308096 | bytes 51645532 | solution.py:105
  73.2 4.0 %fusion.8 = f32[512,2048]{1,0:T(8,128)S(1)} fusion(f32[4,512,2048]{2,1,0:T(8,128)} %get-tuple-element.178, s32[]{:T(128)S(6)} %select_n.61, s32[]{:T(128)S(6)} %max.7, f32[512]{0:T(512)S(1)} %bitcast.135, f32[]{:T(128)S(6)} %convert_element_type.67), kind=kLoop, calls=%fused_computation.15 | loop fusion | flops 3145728 | bytes 12584972 | tf_op jit(solution)/shard_map/while/body/eval_jaxpr/cond/branch_1_fun/add | solution.py:77
  81.7 5.2 %maximum_add_fusion.1 = f32[512,2048]{1,0:T(8,128)} fusion(f32[512,2048]{1,0:T(8,128)} %get-tuple-element.177, f32[256,2048]{1,0:T(8,128)S(1)} %get-tuple-element.259, f32[256,2048]{1,0:T(8,128)S(1)} %get-tuple-element.258), kind=kLoop, calls=%fused_computation.13 | loop fusion | flops 2097152 | bytes 12582912 | tf_op jit(solution)/shard_map/while/body/eval_jaxpr/cond/branch_1_fun/add | solution.py:101
  92.0 13.8 %conditional.5 = (f32[512,2048]{1,0:T(8,128)}) conditional(s32[]{:T(128)} %convert_element_type.183, f32[512,2048]{1,0:T(8,128)} %get-tuple-element.407, (s32[]{:T(128)}, f32[4,512,2048]{2,1,0:T(8,128)}, f32[512,1]{0,1:T(1,128)S(1)}, bf16[4,128,2048]{2,1,0:T(8,128)(2,1)}, s32[]{:T(128)}, /*index=5*/bf16[512,128]{1,0:T(8,128)(2,1)S(1)}, ...), branch_computations={%region_9.9_spmd, %region_10.10_spmd} | conditional | flops 546308096 | bytes 51645532 | solution.py:105
  92.0 4.0 %fusion.8 = f32[512,2048]{1,0:T(8,128)S(1)} fusion(f32[4,512,2048]{2,1,0:T(8,128)} %get-tuple-element.178, s32[]{:T(128)S(6)} %select_n.61, s32[]{:T(128)S(6)} %max.7, f32[512]{0:T(512)S(1)} %bitcast.135, f32[]{:T(128)S(6)} %convert_element_type.67), kind=kLoop, calls=%fused_computation.15 | loop fusion | flops 3145728 | bytes 12584972 | tf_op jit(solution)/shard_map/while/body/eval_jaxpr/cond/branch_1_fun/add | solution.py:77
  100.6 5.2 %maximum_add_fusion.1 = f32[512,2048]{1,0:T(8,128)} fusion(f32[512,2048]{1,0:T(8,128)} %get-tuple-element.177, f32[256,2048]{1,0:T(8,128)S(1)} %get-tuple-element.259, f32[256,2048]{1,0:T(8,128)S(1)} %get-tuple-element.258), kind=kLoop, calls=%fused_computation.13 | loop fusion | flops 2097152 | bytes 12582912 | tf_op jit(solution)/shard_map/while/body/eval_jaxpr/cond/branch_1_fun/add | solution.py:101
  110.8 13.8 %conditional.5 = (f32[512,2048]{1,0:T(8,128)}) conditional(s32[]{:T(128)} %convert_element_type.183, f32[512,2048]{1,0:T(8,128)} %get-tuple-element.407, (s32[]{:T(128)}, f32[4,512,2048]{2,1,0:T(8,128)}, f32[512,1]{0,1:T(1,128)S(1)}, bf16[4,128,2048]{2,1,0:T(8,128)(2,1)}, s32[]{:T(128)}, /*index=5*/bf16[512,128]{1,0:T(8,128)(2,1)S(1)}, ...), branch_computations={%region_9.9_spmd, %region_10.10_spmd} | conditional | flops 546308096 | bytes 51645532 | solution.py:105
  110.8 4.0 %fusion.8 = f32[512,2048]{1,0:T(8,128)S(1)} fusion(f32[4,512,2048]{2,1,0:T(8,128)} %get-tuple-element.178, s32[]{:T(128)S(6)} %select_n.61, s32[]{:T(128)S(6)} %max.7, f32[512]{0:T(512)S(1)} %bitcast.135, f32[]{:T(128)S(6)} %convert_element_type.67), kind=kLoop, calls=%fused_computation.15 | loop fusion | flops 3145728 | bytes 12584972 | tf_op jit(solution)/shard_map/while/body/eval_jaxpr/cond/branch_1_fun/add | solution.py:77
  119.4 5.2 %maximum_add_fusion.1 = f32[512,2048]{1,0:T(8,128)} fusion(f32[512,2048]{1,0:T(8,128)} %get-tuple-element.177, f32[256,2048]{1,0:T(8,128)S(1)} %get-tuple-element.259, f32[256,2048]{1,0:T(8,128)S(1)} %get-tuple-element.258), kind=kLoop, calls=%fused_computation.13 | loop fusion | flops 2097152 | bytes 12582912 | tf_op jit(solution)/shard_map/while/body/eval_jaxpr/cond/branch_1_fun/add | solution.py:101
  124.7 3.7 %convolution_convert_fusion = bf16[128,2048]{1,0:T(8,128)(2,1)S(1)} fusion(f32[512,2048]{1,0:T(8,128)} %get-tuple-element.203, f32[256,128]{1,0:T(8,128)S(1)} %get-tuple-element.269, f32[256,128]{1,0:T(8,128)} %copy-done.12), kind=kOutput, calls=%fused_computation.27 | convolution fusion | flops 805634048 | bytes 4980736 | tf_op jit(solution)/shard_map/bf,fc->bc/dot_general | solution.py:39
  128.5 2.1 fusion.35
  130.6 11.7 %all-reduce = (f32[128]{0:T(128)S(1)}, f32[128]{0:T(128)S(1)}) all-reduce(f32[128]{0:T(128)S(1)} %copy-done.39, f32[128]{0:T(128)S(1)} %get-tuple-element.205), channel_id=1, replica_groups=mesh['pipe'=2,'seq'=4,'chan'=4] {'chan'}, use_global_device_ids=true, to_apply=%region_1.2 | all-reduce | flops 256 | bytes 2048 | tf_op jit(solution)/shard_map/psum | solution.py:133
  144.0 19.4 %all-gather.3.cloned.1.call-done = bf16[512,2048]{1,0:T(8,128)(2,1)} async-done(((bf16[128,2048]{1,0:T(8,128)(2,1)}), bf16[512,2048]{1,0:T(8,128)(2,1)}) %all-gather.3.cloned.1.call-update) | async-done | bytes 2097168 | tf_op jit(solution)/shard_map/all_gather | solution.py:90
  163.9 2.4 broadcast.110
  166.4 36.6 %while.26 = (s32[]{:T(128)}, f32[512,2048]{1,0:T(8,128)}, s32[4]{0:T(128)}, s32[4]{0:T(128)}, s32[]{:T(128)}, /*index=5*/f32[4,512,2048]{2,1,0:T(8,128)}, f32[51...) while((s32[]{:T(128)}, f32[512,2048]{1,0:T(8,128)}, ...), condition=%wide.region_5.6_spmd, body=%wide.region_2.5_spmd.sunk | while | flops 546308096 | bytes 51645804 | solution.py:108
  172.1 13.8 %conditional.4 = (f32[512,2048]{1,0:T(8,128)}) conditional(s32[]{:T(128)} %convert_element_type.182, f32[512,2048]{1,0:T(8,128)} %get-tuple-element.446, (s32[]{:T(128)}, f32[4,512,2048]{2,1,0:T(8,128)}, f32[512,1]{0,1:T(1,128)S(1)}, bf16[4,128,2048]{2,1,0:T(8,128)(2,1)}, s32[]{:T(128)}, /*index=5*/bf16[512,128]{1,0:T(8,128)(2,1)S(1)}, ...), branch_computations={%region_3.3_spmd, %region_4.4_spmd} | conditional | flops 546308096 | bytes 51645532 | solution.py:105
  172.1 4.0 %fusion = f32[512,2048]{1,0:T(8,128)S(1)} fusion(f32[4,512,2048]{2,1,0:T(8,128)} %get-tuple-element.159, s32[]{:T(128)S(6)} %select_n.59, s32[]{:T(128)S(6)} %max.6, f32[512]{0:T(512)S(1)} %bitcast.136, f32[]{:T(128)S(6)} %convert_element_type.65), kind=kLoop, calls=%fused_computation.2 | loop fusion | flops 3145728 | bytes 12584972 | tf_op jit(solution)/shard_map/while/body/eval_jaxpr/cond/branch_1_fun/add | solution.py:77
  180.6 5.2 %maximum_add_fusion = f32[512,2048]{1,0:T(8,128)} fusion(f32[512,2048]{1,0:T(8,128)} %get-tuple-element.158, f32[256,2048]{1,0:T(8,128)S(1)} %get-tuple-element.257, f32[256,2048]{1,0:T(8,128)S(1)} %get-tuple-element.256), kind=kLoop, calls=%fused_computation | loop fusion | flops 2097152 | bytes 12582912 | tf_op jit(solution)/shard_map/while/body/eval_jaxpr/cond/branch_1_fun/add | solution.py:101
  203.2 3.7 %convolution_convert_fusion.1 = bf16[128,2048]{1,0:T(8,128)(2,1)S(1)} fusion(f32[512,2048]{1,0:T(8,128)} %get-tuple-element.202, f32[256,128]{1,0:T(8,128)} %copy-done.11, f32[256,128]{1,0:T(8,128)S(1)} %copy-done.10), kind=kOutput, calls=%fused_computation.28 | convolution fusion | flops 805699584 | bytes 4980736 | tf_op jit(solution)/shard_map/bf,fc->bc/dot_general | solution.py:39
  207.0 2.4 broadcast_select_fusion
  211.1 52.0 %psum.31 = bf16[1,7,2048]{2,0,1:T(2,128)(2,1)S(1)} all-reduce(bf16[1,7,2048]{2,0,1:T(2,128)(2,1)S(1)} %broadcast_in_dim.32), channel_id=1, replica_groups=mesh['pipe'=2,'seq'=4,'chan'=4] {'seq'}, use_global_device_ids=true, to_apply=%region_21.22 | all-reduce | flops 14336 | bytes 57344 | tf_op jit(solution)/shard_map/psum | solution.py:164
  263.8 2.2 fusion.77
  (152 shorter events, 52.0 us)
Async XLA Ops:
  7.2 22.0 %copy-start = (bf16[1,512,2048]{2,1,0:T(8,128)(2,1)S(1)}, bf16[1,512,2048]{2,1,0:T(8,128)(2,1)}, u32[]{:S(2)}) copy-start(bf16[1,512,2048]{2,1,0:T(8,128)(2,1)} %param.19) | copy-start | bytes 6291460
  7.2 21.3 %copy-start.3 = (bf16[1,128,2048]{2,1,0:T(8,128)(2,1)S(1)}, bf16[1,128,2048]{2,1,0:T(8,128)(2,1)}, u32[]{:S(2)}) copy-start(bf16[1,128,2048]{2,1,0:T(8,128)(2,1)} %param.15) | copy-start | bytes 1572868
  7.2 39.7 %all-gather.5.cloned.1.call-start = ((), (), s32[]{:S(2)}) async-start(), calls=%async_computation.1 | async-start | bytes 2621440 | tf_op jit(solution)/shard_map/all_gather | solution.py:90
  8.8 17.7 %copy-start.15 = (f32[1,1,2048]{2,0,1:T(1,128)}, f32[1,1,2048]{2,0,1:T(1,128)S(1)}, u32[]{:S(2)}) copy-start(f32[1,1,2048]{2,0,1:T(1,128)S(1)} %get-tuple-element.260) | copy-start | bytes 24580
  8.8 17.7 %copy-start.18 = (f32[1,1,2048]{2,0,1:T(1,128)}, f32[1,1,2048]{2,0,1:T(1,128)S(1)}, u32[]{:S(2)}) copy-start(f32[1,1,2048]{2,0,1:T(1,128)S(1)} %get-tuple-element.263) | copy-start | bytes 24580
  25.9 137.5 %all-gather.3.cloned.1.call-start = ((), (), s32[]{:S(2)}) async-start(), calls=%async_computation | async-start | bytes 2621440 | tf_op jit(solution)/shard_map/all_gather | solution.py:90
  27.1 4.5 %copy-start.9 = (f32[256,128]{1,0:T(8,128)}, f32[256,128]{1,0:T(8,128)S(1)}, u32[]{:S(2)}) copy-start(f32[256,128]{1,0:T(8,128)S(1)} %get-tuple-element.267) | copy-start | bytes 393220
  27.1 4.5 %copy-start.11 = (f32[256,128]{1,0:T(8,128)}, f32[256,128]{1,0:T(8,128)S(1)}, u32[]{:S(2)}) copy-start(f32[256,128]{1,0:T(8,128)S(1)} %get-tuple-element.268) | copy-start | bytes 393220
  124.7 5.9 %copy-start.39 = (f32[128]{0:T(128)S(1)}, f32[128]{0:T(128)}, u32[]{:S(2)}) copy-start(f32[128]{0:T(128)} %fusion.37) | copy-start | bytes 1540
  128.3 38.0 %copy-start.5 = (bf16[128,2048]{1,0:T(8,128)(2,1)}, bf16[128,2048]{1,0:T(8,128)(2,1)S(1)}, u32[]{:S(2)}) copy-start(bf16[128,2048]{1,0:T(8,128)(2,1)S(1)} %convolution_convert_fusion) | copy-start | bytes 1572868
  142.2 24.1 %copy-start.34 = (f32[128]{0:T(128)}, f32[128]{0:T(128)S(1)}, u32[]{:S(2)}) copy-start(f32[128]{0:T(128)S(1)} %add_rsqrt_fusion.1) | copy-start | bytes 1540
  166.4 36.7 %copy-start.10 = (f32[256,128]{1,0:T(8,128)S(1)}, f32[256,128]{1,0:T(8,128)}, u32[]{:S(2)}) copy-start(f32[256,128]{1,0:T(8,128)} %copy-done.9) | copy-start | bytes 393220
  203.0 3.9 %copy-start.6 = (bf16[128,2048]{1,0:T(8,128)(2,1)S(1)}, bf16[128,2048]{1,0:T(8,128)(2,1)}, u32[]{:S(2)}) copy-start(bf16[128,2048]{1,0:T(8,128)(2,1)} %copy-done.5) | copy-start | bytes 1572868
  203.0 3.9 %copy-start.8 = (bf16[1,128,2048]{2,1,0:T(8,128)(2,1)S(1)}, bf16[1,128,2048]{2,1,0:T(8,128)(2,1)}, u32[]{:S(2)}) copy-start(bf16[1,128,2048]{2,1,0:T(8,128)(2,1)} %param.18) | copy-start | bytes 1572868
  203.0 3.9 %copy-start.14 = (bf16[1,128,2048]{2,1,0:T(8,128)(2,1)S(1)}, bf16[1,128,2048]{2,1,0:T(8,128)(2,1)}, u32[]{:S(2)}) copy-start(bf16[1,128,2048]{2,1,0:T(8,128)(2,1)} %param.17) | copy-start | bytes 1572868
  203.0 3.9 %copy-start.17 = (f32[1,1,2048]{2,0,1:T(1,128)S(1)}, f32[1,1,2048]{2,0,1:T(1,128)}, u32[]{:S(2)}) copy-start(f32[1,1,2048]{2,0,1:T(1,128)} %copy-done.15) | copy-start | bytes 24580
  203.0 3.9 %copy-start.19 = (f32[1,1,2048]{2,0,1:T(1,128)S(1)}, f32[1,1,2048]{2,0,1:T(1,128)}, u32[]{:S(2)}) copy-start(f32[1,1,2048]{2,0,1:T(1,128)} %copy-done.18) | copy-start | bytes 24580
  203.0 3.9 %copy-start.21 = (f32[1,1,2048]{2,0,1:T(1,128)S(1)}, f32[1,1,2048]{2,0,1:T(1,128)}, u32[]{:S(2)}) copy-start(f32[1,1,2048]{2,0,1:T(1,128)} %get-tuple-element.261) | copy-start | bytes 24580
  203.0 3.9 %copy-start.23 = (f32[1,1,2048]{2,0,1:T(1,128)S(1)}, f32[1,1,2048]{2,0,1:T(1,128)}, u32[]{:S(2)}) copy-start(f32[1,1,2048]{2,0,1:T(1,128)} %get-tuple-element.262) | copy-start | bytes 24580
  203.0 3.9 %copy-start.25 = (f32[1,1,2048]{2,0,1:T(1,128)S(1)}, f32[1,1,2048]{2,0,1:T(1,128)}, u32[]{:S(2)}) copy-start(f32[1,1,2048]{2,0,1:T(1,128)} %get-tuple-element.265) | copy-start | bytes 24580
  203.0 3.9 %copy-start.27 = (f32[1,1,2048]{2,0,1:T(1,128)S(1)}, f32[1,1,2048]{2,0,1:T(1,128)}, u32[]{:S(2)}) copy-start(f32[1,1,2048]{2,0,1:T(1,128)} %get-tuple-element.266) | copy-start | bytes 24580
  203.1 3.9 %copy-start.35 = (f32[128]{0:T(128)S(1)}, f32[128]{0:T(128)}, u32[]{:S(2)}) copy-start(f32[128]{0:T(128)} %copy-done.34) | copy-start | bytes 1540
  203.1 3.9 %copy-start.38 = (f32[128]{0:T(128)S(1)}, f32[128]{0:T(128)}, u32[]{:S(2)}) copy-start(f32[128]{0:T(128)} %copy-done.36) | copy-start | bytes 1540
  203.1 3.9 %copy-start.40 = (f32[128]{0:T(128)S(1)}, f32[128]{0:T(128)}, u32[]{:S(2)}) copy-start(f32[128]{0:T(128)} %broadcast_multiply_fusion) | copy-start | bytes 1540
  203.1 7.7 %copy-start.33 = (bf16[2048]{0:T(1024)(128)(2,1)S(1)}, bf16[2048]{0:T(1024)(128)(2,1)}, u32[]{:S(2)}) copy-start(bf16[2048]{0:T(1024)(128)(2,1)} %get-tuple-element.204) | copy-start | bytes 12292
  203.1 7.7 %copy-start.32 = (bf16[2048]{0:T(1024)(128)(2,1)S(1)}, bf16[2048]{0:T(1024)(128)(2,1)}, u32[]{:S(2)}) copy-start(bf16[2048]{0:T(1024)(128)(2,1)} %get-tuple-element.206) | copy-start | bytes 12292
  203.1 7.8 %copy-start.31 = (bf16[2048]{0:T(1024)(128)(2,1)S(1)}, bf16[2048]{0:T(1024)(128)(2,1)}, u32[]{:S(2)}) copy-start(bf16[2048]{0:T(1024)(128)(2,1)} %get-tuple-element.211) | copy-start | bytes 12292
  203.1 7.8 %copy-start.30 = (bf16[2048]{0:T(1024)(128)(2,1)S(1)}, bf16[2048]{0:T(1024)(128)(2,1)}, u32[]{:S(2)}) copy-start(bf16[2048]{0:T(1024)(128)(2,1)} %get-tuple-element.208) | copy-start | bytes 12292
  203.1 7.8 %copy-start.29 = (bf16[2048]{0:T(1024)(128)(2,1)S(1)}, bf16[2048]{0:T(1024)(128)(2,1)}, u32[]{:S(2)}) copy-start(bf16[2048]{0:T(1024)(128)(2,1)} %get-tuple-element.209) | copy-start | bytes 12292
  203.1 7.8 %copy-start.28 = (bf16[2048]{0:T(1024)(128)(2,1)S(1)}, bf16[2048]{0:T(1024)(128)(2,1)}, u32[]{:S(2)}) copy-start(bf16[2048]{0:T(1024)(128)(2,1)} %get-tuple-element.210) | copy-start | bytes 12292
  203.2 63.7 %copy-start.1 = (bf16[1,512,2048]{2,1,0:T(8,128)(2,1)S(1)}, bf16[1,512,2048]{2,1,0:T(8,128)(2,1)}, u32[]{:S(2)}) copy-start(bf16[1,512,2048]{2,1,0:T(8,128)(2,1)} %param.19) | copy-start | bytes 6291460
  209.4 56.7 %collective-permute-start = (bf16[128,2048]{1,0:T(8,128)(2,1)}, bf16[128,2048]{1,0:T(8,128)(2,1)S(1)}, u32[]{:S(2)}, u32[]{:S(2)}) collective-permute-start(bf16[128,2048]{1,0:T(8,128)(2,1)} %get-tuple-element.254), channel_id=1, source_target_pairs={{0,16},{16,0},{1,17},{17,1},{2,18},{18,2},{3,19},{19,3},{4,20},{20... | collective-permute-start | bytes 1572872 | tf_op jit(solution)/shard_map/ppermute | solution.py:21
  (12 other events, 42.0 us)
Sparse Core Ops, SparseCore 0:
  26.0 20.7 all-gather.4
  143.5 19.8 all-gather.2
where the time goes:
time: 275 us; the launch traced here: 274 us
  blocking collectives  77.1 us (28%)
  other arithmetic  65.7 us (24%)
  matrix products  35.4 us (13%)
  local copies, waits for them, and re-layouts  27.1 us (10%)
  waiting for transfers between devices  26.5 us (10%)
  loops' own time  25.6 us (9%)
  between operations  14.7 us (5%)
    psum x1, blocking collectives, per_device(): param_grad = lax.psum(rows.astype(jnp.bfloat16), 'seq').astype(jnp.float32)  52 us
    all_gather x2, waiting for transfers between devices, cycle_conv(): lax.all_gather(signal, 'seq', axis=0, tiled=True)  26.5 us
    add x5, other arithmetic, add_term(): inner_sum + spectral_product(lagged_spectrum(spectra, parity_rows, distan...  26.1 us
    another operation x2, loops' own time, cycle_conv(): lax.scan(one_block, running_sum, (arrived_blocks, offsets))  25.3 us
    psum x2, blocking collectives, per_device(): lax.psum((jnp.sum(inputs * inputs, axis=1), jnp.sum(saved * saved, axis=1...  25.1 us
    add x5, other arithmetic, lagged_spectrum(): return earlier * (distance > 0).astype(jnp.float32) + parity_rows * current  20 us
    dot_general x6, matrix products, table_apply(): jnp.einsum(form, low_part, data, preferred_element_type=jnp.float32)  17 us
    dot_general x6, matrix products, table_apply(): jnp.einsum(form, high_part, data, preferred_element_type=jnp.float32)  11 us
  transfers between devices with their start and end apart: 3, of which 2 were waited for; matrix products, arithmetic and copies ran while one was open for 6% of the time, Pallas kernels for 0%

commit v1 on v0

v1 whole, which is shorter than its diff:
```python
import functools

import jax
import jax.numpy as jnp
import numpy as np
from jax import lax
from jax.experimental import pallas as pl
from jax.experimental.pallas import tpu as pltpu
from jax.sharding import PartitionSpec as P

EPSILON = 1e-05
MESH = pl.DeviceIdType.MESH


def transform_tables(rows):
    period = 2 * rows
    angle = (
        2.0 * np.pi / period * (np.arange(rows)[:, None] + 0.5) * np.arange(period)[None, :]
    )
    forward = np.concatenate([np.cos(angle), -np.sin(angle)], axis=0)
    inverse = (forward[:, rows:] / rows).T
    enter = np.stack([forward[:, :rows], inverse.T])
    leave = np.stack([inverse, forward[:, :rows].T])
    return tuple(jnp.asarray(t, jnp.bfloat16) for t in (forward, enter, leave))


def fold_lanes(values):
    lanes = 128
    total = values[:, :lanes]
    for at in range(lanes, values.shape[1], lanes):
        total = total + values[:, at : at + lanes]
    return total


def widen(column, width):
    return jnp.concatenate([column] * (width // column.shape[1]), axis=1)


def kernel(
    sizes,
    order,
    fwd_in,
    saved_in,
    saved_conv,
    grad_out,
    filters,
    params,
    forward_tab,
    enter_tab,
    leave_tab,
    layer_out,
    input_grad,
    param_grad,
    received,
    own_all,
    grad_all,
    spectra,
    grad_normed,
    column_all,
    saved_column,
    cross_lanes,
    square_rows,
    rms_rows,
    cross_rows,
    sum_rows,
    load_sem,
    send_sem,
    recv_sem,
    square_sem,
    rms_sem,
    cross_sem,
    sum_sem,
    relay_sem,
):
    n_seq, n_chan, channels, chunks = sizes
    rows, slab = saved_in.shape
    width = slab // chunks
    chips = n_seq // 2
    me = lax.axis_index("seq")
    my_chan = lax.axis_index("chan")
    pipe = lax.axis_index("pipe")
    chip, core = me // 2, me % 2
    sibling = chip * 2 + 1 - core

    def columns(c):
        return pl.ds(pl.multiple_of(c * width, width), width)

    def same_core(j):
        return lax.rem(chip + j, chips) * 2 + core

    def other_core(j):
        return lax.rem(chip + j, chips) * 2 + 1 - core

    def block_copy(kind, slot, c, k, target):
        buffer = own_all if kind == 0 else grad_all
        return pltpu.make_async_remote_copy(
            src_ref=buffer.at[slot, :, columns(c)],
            dst_ref=buffer.at[slot, :, columns(c)],
            send_sem=send_sem.at[kind, k, c],
            recv_sem=recv_sem.at[kind, slot, c],
            device_id={"seq": target},
            device_id_type=MESH,
        )

    def own_copies(kind, c):
        found = [block_copy(kind, me, c, j, same_core(j)) for j in range(1, chips)]
        return found + [block_copy(kind, me, c, 0, sibling)]

    def relay_copies(kind, c):
        return [
            block_copy(kind, same_core(j), c, chips - 1 + j, sibling) for j in range(1, chips)
        ]

    def start_own(kind, c):
        for copy in own_copies(kind, c):
            copy.start()

    def relay(kind, c):
        for j, copy in enumerate(relay_copies(kind, c)):
            block_copy(kind, same_core(j + 1), c, 0, sibling).wait_recv()
            copy.start()

    def arrive(kind, slot, c):
        block_copy(kind, slot, c, 0, sibling).wait_recv()

    def small_copies(buffer, sems, axis, index, count):
        return [
            pltpu.make_async_remote_copy(
                src_ref=buffer.at[index],
                dst_ref=buffer.at[index],
                send_sem=sems.at[0, j],
                recv_sem=sems.at[1, index],
                device_id={axis: lax.rem(index + j, count)},
                device_id_type=MESH,
            )
            for j in range(1, count)
        ]

    def small_wait(buffer, sems, axis, index, count):
        for j in range(1, count):
            peer = lax.rem(index + j, count)
            pltpu.make_async_remote_copy(
                src_ref=buffer.at[peer],
                dst_ref=buffer.at[peer],
                send_sem=sems.at[0, j],
                recv_sem=sems.at[1, peer],
                device_id={axis: peer},
                device_id_type=MESH,
            ).wait_recv()

    def partner_copy(source, c):
        return pltpu.make_async_remote_copy(
            src_ref=source.at[:, columns(c)],
            dst_ref=received.at[:, columns(c)],
            send_sem=relay_sem.at[0, c],
            recv_sem=relay_sem.at[1, c],
            device_id={"pipe": 1 - pipe},
            device_id_type=MESH,
        )

    def load_copy(c):
        return pltpu.make_async_copy(
            fwd_in.at[:, columns(c)], own_all.at[me, :, columns(c)], load_sem.at[c]
        )

    for c in range(chunks):
        load_copy(c).start()

    barrier = pltpu.get_barrier_semaphore()
    for j in range(1, n_seq):
        pl.semaphore_signal(
            barrier, inc=1, device_id={"seq": lax.rem(me + j, n_seq)}, device_id_type=MESH
        )
    for j in range(1, n_chan):
        pl.semaphore_signal(
            barrier, inc=1, device_id={"chan": lax.rem(my_chan + j, n_chan)}, device_id_type=MESH
        )
    pl.semaphore_signal(barrier, inc=1, device_id={"pipe": 1 - pipe}, device_id_type=MESH)
    pl.semaphore_wait(barrier, n_seq + n_chan - 1)

    early = chunks // 2
    for c in range(chunks):
        load_copy(c).wait()
        if c < early:
            start_own(0, c)

    def squares(read):
        def step(c, total):
            part = read(c).astype(jnp.float32)
            return total + fold_lanes(part * part)

        lanes = lax.fori_loop(0, chunks, step, jnp.zeros((rows, 128), jnp.float32))
        return jnp.sum(lanes.T, axis=0, keepdims=True)

    saved_row = squares(lambda c: saved_in[:, columns(c)])
    fwd_row = squares(lambda c: own_all[me, :, columns(c)])
    square_rows[my_chan] = jnp.concatenate([fwd_row, saved_row] * 4, axis=0)
    for copy in small_copies(square_rows, square_sem, "chan", my_chan, n_chan):
        copy.start()

    def filter_step(c, carry):
        cols = columns(c)
        spectra[0, :, cols] = jnp.zeros((2 * rows, width), jnp.bfloat16)
        spectra[1, :, cols] = jnp.dot(
            forward_tab[:, rows:], filters[:rows, cols], preferred_element_type=jnp.float32
        ).astype(jnp.bfloat16)

        def window(d, inner):
            taps = filters[pl.ds(pl.multiple_of((d - 1) * rows, rows), 2 * rows), cols]
            spectra[d + 1, :, cols] = jnp.dot(
                forward_tab[...], taps, preferred_element_type=jnp.float32
            ).astype(jnp.bfloat16)
            return inner

        return lax.fori_loop(1, n_seq, window, carry)

    lax.fori_loop(0, chunks, filter_step, 0)

    small_wait(square_rows, square_sem, "chan", my_chan, n_chan)
    total_squares = square_rows[0]
    for j in range(1, n_chan):
        total_squares = total_squares + square_rows[j]
    inv_rows = lax.rsqrt(total_squares / channels + EPSILON)
    rms_rows[me] = inv_rows
    for copy in small_copies(rms_rows, rms_sem, "seq", me, n_seq):
        copy.start()
    saved_column[...] = jnp.broadcast_to(inv_rows[1:2], (rows, rows)).T

    def param(index, cols):
        return params[index : index + 1, cols]

    def grad_conv_step(c, carry):
        cols = columns(c)
        scaled = (
            saved_in[:, cols].astype(jnp.float32) * widen(saved_column[...], width) * param(0, cols)
        )
        query = scaled * param(1, cols) + param(2, cols)
        grad_all[me, :, cols] = (grad_out[:, cols].astype(jnp.float32) * query).astype(jnp.bfloat16)
        start_own(1, c)
        return carry

    lax.fori_loop(0, chunks, grad_conv_step, 0)

    small_wait(rms_rows, rms_sem, "seq", me, n_seq)
    for s in range(n_seq):
        column_all[s] = jnp.broadcast_to(rms_rows[s, 0:1], (rows, rows)).T

    my_position = order[me]

    def long_conv(kind, c, signal):
        cols = columns(c)

        def term(slot, sums):
            distance = my_position - order[slot] if kind == 0 else order[slot] - my_position
            entering = jnp.dot(
                enter_tab[kind], signal(slot), preferred_element_type=jnp.float32
            )
            window = spectra[jnp.maximum(distance, -1) + 1, :, cols].astype(jnp.float32)
            data_real, data_imag = entering[:rows], entering[rows:]
            tap_real, tap_imag = window[:rows], window[rows:]
            if kind == 0:
                real = tap_real * data_real - tap_imag * data_imag
                imag = tap_real * data_imag + tap_imag * data_real
            else:
                real = tap_real * data_real + tap_imag * data_imag
                imag = tap_real * data_imag - tap_imag * data_real
            if sums is None:
                return real, imag
            return sums[0] + real, sums[1] + imag

        sums = term(me, None)
        arrive(kind, sibling, c)
        sums = term(sibling, sums)
        for j in range(1, chips):
            sums = term(same_core(j), sums)
        for j in range(1, chips):
            arrive(kind, other_core(j), c)
            sums = term(other_core(j), sums)
        spectrum = jnp.concatenate(sums, axis=0).astype(jnp.bfloat16)
        return jnp.dot(leave_tab[kind], spectrum, preferred_element_type=jnp.float32).astype(
            jnp.bfloat16
        )

    def backward_step(c, carry):
        cols = columns(c)
        relay(1, c)
        grad_mixed = long_conv(1, c, lambda slot: grad_all[slot, :, cols]).astype(jnp.float32)
        normed = saved_in[:, cols].astype(jnp.float32) * widen(saved_column[...], width)
        scaled = normed * param(0, cols)
        key = scaled * param(3, cols) + param(4, cols)
        value = scaled * param(5, cols) + param(6, cols)
        grad_query = grad_out[:, cols].astype(jnp.float32) * saved_conv[:, cols].astype(jnp.float32)
        grad_key = grad_mixed * value
        grad_value = grad_mixed * key
        grad_scaled = (
            grad_query * param(1, cols) + grad_key * param(3, cols) + grad_value * param(5, cols)
        )
        terms = [
            grad_scaled * normed,
            grad_query * scaled,
            grad_query,
            grad_key * scaled,
            grad_key,
            grad_value * scaled,
            grad_value,
        ]
        sums = [jnp.sum(term, axis=0, keepdims=True) for term in terms]
        sum_rows[me, :, cols] = jnp.concatenate(sums + sums[:1], axis=0)
        outer = grad_scaled * param(0, cols)
        grad_normed[:, cols] = outer
        cross_lanes[...] += fold_lanes(outer * normed)
        return carry

    cross_lanes[...] = jnp.zeros_like(cross_lanes)
    for c in range(early):
        relay(0, c)
    lax.fori_loop(0, early, backward_step, 0)
    for c in range(early, chunks):
        start_own(0, c)
    lax.fori_loop(early, chunks, backward_step, 0)

    cross_rows[my_chan] = jnp.broadcast_to(
        jnp.sum(cross_lanes[...].T, axis=0, keepdims=True), (8, rows)
    )
    for copy in small_copies(cross_rows, cross_sem, "chan", my_chan, n_chan):
        copy.start()
    for copy in small_copies(sum_rows, sum_sem, "seq", me, n_seq):
        copy.start()

    def forward_step(c, carry):
        cols = columns(c)

        def mixed(slot):
            scaled = (
                own_all[slot, :, cols].astype(jnp.float32)
                * widen(column_all[slot], width)
                * param(0, cols)
            )
            key = scaled * param(3, cols) + param(4, cols)
            value = scaled * param(5, cols) + param(6, cols)
            return (key * value).astype(jnp.bfloat16)

        conv = long_conv(0, c, mixed).astype(jnp.float32)
        inputs = own_all[me, :, cols].astype(jnp.float32)
        scaled = inputs * widen(column_all[me], width) * param(0, cols)
        query = scaled * param(1, cols) + param(2, cols)
        layer_out[:, cols] = (inputs + query * conv).astype(jnp.bfloat16)

        @pl.when(pipe == 0)
        def _():
            partner_copy(layer_out, c).start()

        return carry

    lax.fori_loop(0, early, forward_step, 0)

    small_wait(cross_rows, cross_sem, "chan", my_chan, n_chan)
    cross = cross_rows[0]
    for j in range(1, n_chan):
        cross = cross + cross_rows[j]
    cross_lanes[...] = jnp.broadcast_to(cross[0:1] / channels, (rows, rows)).T

    def input_grad_step(c, carry):
        cols = columns(c)
        inverse = widen(saved_column[...], width)
        normed = saved_in[:, cols].astype(jnp.float32) * inverse
        inner = grad_normed[:, cols] - normed * widen(cross_lanes[...], width)
        input_grad[:, cols] = (
            grad_out[:, cols].astype(jnp.float32) + inverse * inner
        ).astype(jnp.bfloat16)

        @pl.when(pipe == 1)
        def _():
            partner_copy(input_grad, c).start()

        return carry

    lax.fori_loop(0, chunks, input_grad_step, 0)

    for c in range(early, chunks):
        relay(0, c)
    lax.fori_loop(early, chunks, forward_step, 0)

    small_wait(sum_rows, sum_sem, "seq", me, n_seq)
    total = sum_rows[0]
    for s in range(1, n_seq):
        total = total + sum_rows[s]
    param_grad[...] = total[: param_grad.shape[0]]

    for c in range(chunks):
        for kind in range(2):
            for copy in own_copies(kind, c) + relay_copies(kind, c):
                copy.wait_send()
    for buffer, sems, axis, index, count in (
        (square_rows, square_sem, "chan", my_chan, n_chan),
        (cross_rows, cross_sem, "chan", my_chan, n_chan),
        (rms_rows, rms_sem, "seq", me, n_seq),
        (sum_rows, sum_sem, "seq", me, n_seq),
    ):
        for copy in small_copies(buffer, sems, axis, index, count):
            copy.wait_send()
    for c in range(chunks):
        partner_copy(layer_out, c).wait()


def per_device(n_seq, n_chan, fwd_in, saved_in, saved_conv, grad_out, filters, mix_params, order):
    rows, slab = fwd_in.shape[1:]
    chunks = 4
    sizes = (n_seq, n_chan, slab * n_chan, chunks)
    n_params = mix_params.shape[1]
    block = jax.ShapeDtypeStruct((rows, slab), jnp.bfloat16)
    vmem = pl.BlockSpec(memory_space=pltpu.VMEM)
    dma = pltpu.SemaphoreType.DMA
    outs = pl.pallas_call(
        functools.partial(kernel, sizes),
        out_shape=(block, block, jax.ShapeDtypeStruct((n_params, slab), jnp.float32), block),
        in_specs=[pl.BlockSpec(memory_space=pltpu.SMEM), pl.BlockSpec(memory_space=pl.ANY)]
        + [vmem] * 8,
        out_specs=(vmem,) * 4,
        scratch_shapes=[
            pltpu.VMEM((n_seq, rows, slab), jnp.bfloat16),
            pltpu.VMEM((n_seq, rows, slab), jnp.bfloat16),
            pltpu.VMEM((n_seq + 1, 2 * rows, slab), jnp.bfloat16),
            pltpu.VMEM((rows, slab), jnp.float32),
            pltpu.VMEM((n_seq, rows, 128), jnp.float32),
            pltpu.VMEM((rows, 128), jnp.float32),
            pltpu.VMEM((rows, 128), jnp.float32),
            pltpu.VMEM((n_chan, 8, rows), jnp.float32),
            pltpu.VMEM((n_seq, 8, rows), jnp.float32),
            pltpu.VMEM((n_chan, 8, rows), jnp.float32),
            pltpu.VMEM((n_seq, 8, slab), jnp.float32),
            dma((chunks,)),
            dma((2, n_seq, chunks)),
            dma((2, n_seq, chunks)),
            dma((2, n_chan)),
            dma((2, n_seq)),
            dma((2, n_chan)),
            dma((2, n_seq)),
            dma((2, chunks)),
        ],
        compiler_params=pltpu.CompilerParams(
            collective_id=0, has_side_effects=True, vmem_limit_bytes=60 * 2**20
        ),
    )(
        order,
        fwd_in[0],
        saved_in[0],
        saved_conv[0],
        grad_out[0],
        filters[0],
        mix_params[0],
        *transform_tables(rows),
    )
    layer_out, input_grad, param_grad, received = outs
    return (layer_out[None], input_grad[None], param_grad[None], received[None])


def solution(mesh):
    spread = P("pipe", "seq", "chan")
    shared = P("pipe", None, "chan")
    return jax.shard_map(
        functools.partial(per_device, mesh.shape["seq"], mesh.shape["chan"]),
        mesh=mesh,
        in_specs=(spread, spread, spread, spread, shared, shared, P()),
        out_specs=(spread, spread, shared, spread),
        check_vma=False,
    )
```

time: 275 us -> 56.4 us (0.21)
  blocking collectives: 77.1 us -> 0 us
  other arithmetic: 65.7 us -> 0 us
  Pallas kernels: 0 us -> 47.8 us
  matrix products: 35.4 us -> 0 us
  waiting for transfers between devices: 26.5 us -> 0 us
  loops' own time: 25.6 us -> 0 us
  local copies, waits for them, and re-layouts: 27.1 us -> 7.61 us
  between operations: 14.7 us -> 0.65 us
    psum x3 -> x0, blocking collectives: 77.1 us -> none  [the longest x1 52 us: per_device(): param_grad = lax.psum(rows.astype(jnp.bfloat16), 'seq').astype(jnp.float32)]
    add x15 -> x0, other arithmetic: 50.2 us -> none  [the longest x5 26.1 us: add_term(): inner_sum + spectral_product(lagged_spectrum(spectra, parity_rows, distan...]
    pallas_call x0 -> x1, Pallas kernels: none -> 47.8 us  [per_device(): pl.pallas_call(functools.partial(kernel, sizes), out_shape=(block, block,...]
    dot_general x14 -> x0, matrix products: 35.4 us -> none  [the longest x6 17 us: table_apply(): jnp.einsum(form, low_part, data, preferred_element_type=jnp.float32)]
    all_gather x2 -> x0, waiting for transfers between devices: 26.5 us -> none  [cycle_conv(): lax.all_gather(signal, 'seq', axis=0, tiled=True)]
    another operation x10 -> x0, loops' own time: 25.6 us -> none  [the longest x2 25.3 us: cycle_conv(): lax.scan(one_block, running_sum, (arrived_blocks, offsets))]
    dynamic_slice x17 -> x0, local copies, waits for them, and re-layouts: 18.9 us -> none  [the longest x8 10.1 us: one_block(): source_position = span_order[offset]]
    unnamed x83 -> x7, local copies, waits for them, and re-layouts: 0.99 us -> 7.61 us
  transfers between devices with their start and end apart: 3 -> 0, of which waited for: 2 -> 0; matrix products, arithmetic and copies ran while one was open for 6% -> 0% of each run, Pallas kernels for 0% -> 0%
where the time goes in v1:
time: 56.4 us; the launch traced here: 56.1 us
  Pallas kernels  47.8 us (85%)
  local copies, waits for them, and re-layouts  7.61 us (13%)
  between operations  0.65 us (1%)
    pallas_call x1, Pallas kernels, per_device(): pl.pallas_call(functools.partial(kernel, sizes), out_shape=(block, block,...  47.8 us
    unnamed x7, local copies, waits for them, and re-layouts  7.61 us

profile of v1, /device:TPU:0, one launch (start us, length us, event | category | flops | bytes accessed | tf_op | source)
XLA Modules:
  0.0 56.1 jit_solution(16655655886593922823)
XLA Ops:
  0.6 1.5 %copy.17 = f32[1,7,2048]{2,1,0:T(8,128)} copy(f32[1,7,2048]{2,0,1:T(1,128)} %param.15) | data formatting | bytes 114688
  2.1 47.8 %shard_map.129 = (bf16[128,2048]{1,0:T(8,128)(2,1)}, bf16[128,2048]{1,0:T(8,128)(2,1)}, f32[7,2048]{1,0:T(8,128)}, bf16[128,2048]{1,0:T(8,128)(2,1)}) custom-call(s32[4]{0:T(128)} %order.1, bf16[128,2048]{1,0:T(8,128)(2,1)} %bitcast.13, bf16[128,2048]{1,0:T(8,128)(2,1)} %bitcast.14, bf16[128,2048]{1,0:T(8,128)(2,1)} %bitcast.15, bf16[128,2048]{1,0:T(8,128)(2,1)} %bitcast.16, ...), custom_call_target="tpu_custom_call" | custom-call | tf_op jit(solution)/shard_map/pallas_call | solution.py:414
  49.9 0.0 copy-start
  50.0 1.6 %copy.14 = f32[1,7,2048]{2,0,1:T(1,128)} copy(f32[1,7,2048]{2,1,0:T(8,128)} %bitcast.21) | data formatting | bytes 114688
  51.5 1.9 %copy.21 = bf16[1,128,2048]{2,1,0:T(8,128)(2,1)} copy(bf16[1,128,2048]{2,1,0:T(8,128)(2,1)} %bitcast.19) | data formatting | bytes 1048576
  53.4 1.9 %copy.22 = bf16[1,128,2048]{2,1,0:T(8,128)(2,1)} copy(bf16[1,128,2048]{2,1,0:T(8,128)(2,1)} %bitcast.18) | data formatting | bytes 1048576
  55.3 0.0 copy-done
  55.3 0.8 %copy.23 = bf16[1,128,2048]{2,1,0:T(8,128)(2,1)} copy(bf16[1,128,2048]{2,1,0:T(8,128)(2,1)S(1)} %bitcast.17) | data formatting | bytes 1048576
Async XLA Ops:
  49.9 5.4 %copy-start = (bf16[128,2048]{1,0:T(8,128)(2,1)S(1)}, bf16[128,2048]{1,0:T(8,128)(2,1)}, u32[]{:S(2)}) copy-start(bf16[128,2048]{1,0:T(8,128)(2,1)} %get-tuple-element.11) | copy-start | bytes 1572868

commit v2 on v1

--- a/solution.py
+++ b/solution.py
@@ -40,10 +40,10 @@
     sizes,
     order,
     fwd_in,
-    saved_in,
-    saved_conv,
-    grad_out,
-    filters,
+    saved_in_hbm,
+    saved_conv_hbm,
+    grad_out_hbm,
+    filters_hbm,
     params,
     forward_tab,
     enter_tab,
@@ -52,6 +52,10 @@
     input_grad,
     param_grad,
     received,
+    saved_in,
+    saved_conv,
+    grad_out,
+    filters,
     own_all,
     grad_all,
     spectra,
@@ -64,6 +68,7 @@
     cross_rows,
     sum_rows,
     load_sem,
+    operand_sem,
     send_sem,
     recv_sem,
     square_sem,
@@ -163,8 +168,21 @@
             fwd_in.at[:, columns(c)], own_all.at[me, :, columns(c)], load_sem.at[c]
         )
 
+    operands = [
+        pltpu.make_async_copy(source, target, operand_sem.at[i])
+        for i, (source, target) in enumerate(
+            (
+                (saved_in_hbm, saved_in),
+                (filters_hbm, filters),
+                (grad_out_hbm, grad_out),
+                (saved_conv_hbm, saved_conv),
+            )
+        )
+    ]
     for c in range(chunks):
         load_copy(c).start()
+    for copy in operands:
+        copy.start()
 
     barrier = pltpu.get_barrier_semaphore()
     for j in range(1, n_seq):
@@ -192,8 +210,9 @@
         lanes = lax.fori_loop(0, chunks, step, jnp.zeros((rows, 128), jnp.float32))
         return jnp.sum(lanes.T, axis=0, keepdims=True)
 
+    fwd_row = squares(lambda c: own_all[me, :, columns(c)])
+    operands[0].wait()
     saved_row = squares(lambda c: saved_in[:, columns(c)])
-    fwd_row = squares(lambda c: own_all[me, :, columns(c)])
     square_rows[my_chan] = jnp.concatenate([fwd_row, saved_row] * 4, axis=0)
     for copy in small_copies(square_rows, square_sem, "chan", my_chan, n_chan):
         copy.start()
@@ -214,6 +233,7 @@
 
         return lax.fori_loop(1, n_seq, window, carry)
 
+    operands[1].wait()
     lax.fori_loop(0, chunks, filter_step, 0)
 
     small_wait(square_rows, square_sem, "chan", my_chan, n_chan)
@@ -227,7 +247,7 @@
     saved_column[...] = jnp.broadcast_to(inv_rows[1:2], (rows, rows)).T
 
     def param(index, cols):
-        return params[index : index + 1, cols]
+        return params[index, :, cols]
 
     def grad_conv_step(c, carry):
         cols = columns(c)
@@ -239,7 +259,9 @@
         start_own(1, c)
         return carry
 
+    operands[2].wait()
     lax.fori_loop(0, chunks, grad_conv_step, 0)
+    operands[3].wait()
 
     small_wait(rms_rows, rms_sem, "seq", me, n_seq)
     for s in range(n_seq):
@@ -385,7 +407,8 @@
     total = sum_rows[0]
     for s in range(1, n_seq):
         total = total + sum_rows[s]
-    param_grad[...] = total[: param_grad.shape[0]]
+    for i in range(param_grad.shape[0]):
+        param_grad[i] = total[i : i + 1]
 
     for c in range(chunks):
         for kind in range(2):
@@ -403,6 +426,28 @@
         partner_copy(layer_out, c).wait()
 
 
+def store_kernel(count, *refs):
+    copies = [
+        pltpu.make_async_copy(refs[i], refs[count + i], refs[2 * count].at[i]) for i in range(count)
+    ]
+    for copy in copies:
+        copy.start()
+    for copy in copies:
+        copy.wait()
+
+
+def store(*arrays):
+    count = len(arrays)
+    anywhere = pl.BlockSpec(memory_space=pl.ANY)
+    return pl.pallas_call(
+        functools.partial(store_kernel, count),
+        out_shape=tuple(jax.ShapeDtypeStruct(a.shape, a.dtype) for a in arrays),
+        in_specs=[anywhere] * count,
+        out_specs=(anywhere,) * count,
+        scratch_shapes=[pltpu.SemaphoreType.DMA((count,))],
+    )(*arrays)
+
+
 def per_device(n_seq, n_chan, fwd_in, saved_in, saved_conv, grad_out, filters, mix_params, order):
     rows, slab = fwd_in.shape[1:]
     chunks = 4
@@ -413,11 +458,16 @@
     dma = pltpu.SemaphoreType.DMA
     outs = pl.pallas_call(
         functools.partial(kernel, sizes),
-        out_shape=(block, block, jax.ShapeDtypeStruct((n_params, slab), jnp.float32), block),
-        in_specs=[pl.BlockSpec(memory_space=pltpu.SMEM), pl.BlockSpec(memory_space=pl.ANY)]
-        + [vmem] * 8,
+        out_shape=(block, block, jax.ShapeDtypeStruct((n_params, 1, slab), jnp.float32), block),
+        in_specs=[pl.BlockSpec(memory_space=pltpu.SMEM)]
+        + [pl.BlockSpec(memory_space=pl.ANY)] * 5
+        + [vmem] * 4,
         out_specs=(vmem,) * 4,
         scratch_shapes=[
+            pltpu.VMEM((rows, slab), jnp.bfloat16),
+            pltpu.VMEM((rows, slab), jnp.bfloat16),
+            pltpu.VMEM((rows, slab), jnp.bfloat16),
+            pltpu.VMEM(filters.shape[1:], jnp.bfloat16),
             pltpu.VMEM((n_seq, rows, slab), jnp.bfloat16),
             pltpu.VMEM((n_seq, rows, slab), jnp.bfloat16),
             pltpu.VMEM((n_seq + 1, 2 * rows, slab), jnp.bfloat16),
@@ -430,6 +480,7 @@
             pltpu.VMEM((n_chan, 8, rows), jnp.float32),
             pltpu.VMEM((n_seq, 8, slab), jnp.float32),
             dma((chunks,)),
+            dma((4,)),
             dma((2, n_seq, chunks)),
             dma((2, n_seq, chunks)),
             dma((2, n_chan)),
@@ -448,11 +499,11 @@
         saved_conv[0],
         grad_out[0],
         filters[0],
-        mix_params[0],
+        mix_params.transpose(1, 0, 2),
         *transform_tables(rows),
     )
-    layer_out, input_grad, param_grad, received = outs
-    return (layer_out[None], input_grad[None], param_grad[None], received[None])
+    layer_out, input_grad, param_grad, received = store(*outs)
+    return (layer_out[None], input_grad[None], param_grad.transpose(1, 0, 2), received[None])
 
 
 def solution(mesh):

time: 56.4 us -> 98.2 us (1.74)
  Pallas kernels: 47.8 us -> 97.4 us
  local copies, waits for them, and re-layouts: 7.61 us -> 0 us
    pallas_call x0 -> x1, Pallas kernels: none -> 50.5 us  [store(): pl.pallas_call(functools.partial(store_kernel, count), out_shape=tuple((j...]
    unnamed x7 -> x0, local copies, waits for them, and re-layouts: 7.61 us -> none
where the time goes in v2:
time: 98.2 us; the launch traced here: 98 us
  Pallas kernels  97.4 us (99%)
    pallas_call x1, Pallas kernels, store(): pl.pallas_call(functools.partial(store_kernel, count), out_shape=tuple((j...  50.5 us
    pallas_call x1, Pallas kernels, per_device(): pl.pallas_call(functools.partial(kernel, sizes), out_shape=(block, block,...  46.9 us

profile of v2, /device:TPU:0, one launch (start us, length us, event | category | flops | bytes accessed | tf_op | source)
XLA Modules:
  0.0 98.0 jit_solution(9219849084732818)
XLA Ops:
  0.6 46.9 %shard_map.129 = (bf16[128,2048]{1,0:T(8,128)(2,1)}, bf16[128,2048]{1,0:T(8,128)(2,1)}, f32[7,1,2048]{2,1,0:T(1,128)}, bf16[128,2048]{1,0:T(8,128)(2,1)}) custom-call(s32[4]{0:T(128)} %order.1, bf16[128,2048]{1,0:T(8,128)(2,1)} %bitcast.11, bf16[128,2048]{1,0:T(8,128)(2,1)} %bitcast.12, bf16[128,2048]{1,0:T(8,128)(2,1)} %bitcast.13, ...), custom_call_target="tpu_custom_call" | custom-call | tf_op jit(solution)/shard_map/pallas_call | solution.py:459
  47.5 50.5 %shard_map.130 = (bf16[128,2048]{1,0:T(8,128)(2,1)}, bf16[128,2048]{1,0:T(8,128)(2,1)}, f32[7,1,2048]{2,1,0:T(1,128)}, bf16[128,2048]{1,0:T(8,128)(2,1)}) custom-call(bf16[128,2048]{1,0:T(8,128)(2,1)} %get-tuple-element.12.refs_0_, bf16[128,2048]{1,0:T(8,128)(2,1)} %get-tuple-element.13.refs_1_, f32[7,1,2048]{2,1,0:T(1,128)} %get-tuple-element.14.refs_2_, ...), custom_call_target="tpu_custom_call" | custom-call | tf_op jit(solution)/shard_map/pallas_call | solution.py:442

commit v3 on v2

--- a/solution.py
+++ b/solution.py
@@ -48,10 +48,12 @@
     forward_tab,
     enter_tab,
     leave_tab,
+    layer_out_hbm,
+    input_grad_hbm,
+    param_grad,
+    received,
     layer_out,
     input_grad,
-    param_grad,
-    received,
     saved_in,
     saved_conv,
     grad_out,
@@ -69,6 +71,7 @@
     sum_rows,
     load_sem,
     operand_sem,
+    result_sem,
     send_sem,
     recv_sem,
     square_sem,
@@ -196,7 +199,8 @@
     pl.semaphore_signal(barrier, inc=1, device_id={"pipe": 1 - pipe}, device_id_type=MESH)
     pl.semaphore_wait(barrier, n_seq + n_chan - 1)
 
-    early = chunks // 2
+    early = chunks // 4
+    middle = chunks // 2
     for c in range(chunks):
         load_copy(c).wait()
         if c < early:
@@ -234,7 +238,7 @@
         return lax.fori_loop(1, n_seq, window, carry)
 
     operands[1].wait()
-    lax.fori_loop(0, chunks, filter_step, 0)
+    lax.fori_loop(0, middle, filter_step, 0)
 
     small_wait(square_rows, square_sem, "chan", my_chan, n_chan)
     total_squares = square_rows[0]
@@ -261,6 +265,7 @@
 
     operands[2].wait()
     lax.fori_loop(0, chunks, grad_conv_step, 0)
+    lax.fori_loop(middle, chunks, filter_step, 0)
     operands[3].wait()
 
     small_wait(rms_rows, rms_sem, "seq", me, n_seq)
@@ -336,10 +341,10 @@
     cross_lanes[...] = jnp.zeros_like(cross_lanes)
     for c in range(early):
         relay(0, c)
-    lax.fori_loop(0, early, backward_step, 0)
+    lax.fori_loop(0, middle, backward_step, 0)
     for c in range(early, chunks):
         start_own(0, c)
-    lax.fori_loop(early, chunks, backward_step, 0)
+    lax.fori_loop(middle, chunks, backward_step, 0)
 
     cross_rows[my_chan] = jnp.broadcast_to(
         jnp.sum(cross_lanes[...].T, axis=0, keepdims=True), (8, rows)
@@ -398,10 +403,22 @@
         return carry
 
     lax.fori_loop(0, chunks, input_grad_step, 0)
-
-    for c in range(early, chunks):
-        relay(0, c)
-    lax.fori_loop(early, chunks, forward_step, 0)
+    stores = [
+        pltpu.make_async_copy(input_grad, input_grad_hbm, result_sem.at[0]),
+        pltpu.make_async_copy(layer_out, layer_out_hbm, result_sem.at[1]),
+    ]
+    stores[0].start()
+
+    def late_forward_step(c, carry):
+        @pl.when(c + 1 < chunks)
+        def _():
+            relay(0, c + 1)
+
+        return forward_step(c, carry)
+
+    relay(0, early)
+    lax.fori_loop(early, chunks, late_forward_step, 0)
+    stores[1].start()
 
     small_wait(sum_rows, sum_sem, "seq", me, n_seq)
     total = sum_rows[0]
@@ -424,15 +441,21 @@
             copy.wait_send()
     for c in range(chunks):
         partner_copy(layer_out, c).wait()
+    for copy in stores:
+        copy.wait()
 
 
 def store_kernel(count, *refs):
-    copies = [
-        pltpu.make_async_copy(refs[i], refs[count + i], refs[2 * count].at[i]) for i in range(count)
-    ]
-    for copy in copies:
-        copy.start()
-    for copy in copies:
+    sources, targets, held = (refs[at * count : (at + 1) * count] for at in range(3))
+    sems = refs[3 * count]
+    fetches = [pltpu.make_async_copy(sources[i], held[i], sems.at[0, i]) for i in range(count)]
+    stores = [pltpu.make_async_copy(held[i], targets[i], sems.at[1, i]) for i in range(count)]
+    for copy in fetches:
+        copy.start()
+    for fetch, copy in zip(fetches, stores):
+        fetch.wait()
+        copy.start()
+    for copy in stores:
         copy.wait()
 
 
@@ -444,26 +467,30 @@
         out_shape=tuple(jax.ShapeDtypeStruct(a.shape, a.dtype) for a in arrays),
         in_specs=[anywhere] * count,
         out_specs=(anywhere,) * count,
-        scratch_shapes=[pltpu.SemaphoreType.DMA((count,))],
+        scratch_shapes=[pltpu.VMEM(a.shape, a.dtype) for a in arrays]
+        + [pltpu.SemaphoreType.DMA((2, count))],
     )(*arrays)
 
 
 def per_device(n_seq, n_chan, fwd_in, saved_in, saved_conv, grad_out, filters, mix_params, order):
     rows, slab = fwd_in.shape[1:]
-    chunks = 4
+    chunks = 8
     sizes = (n_seq, n_chan, slab * n_chan, chunks)
     n_params = mix_params.shape[1]
     block = jax.ShapeDtypeStruct((rows, slab), jnp.bfloat16)
     vmem = pl.BlockSpec(memory_space=pltpu.VMEM)
+    hbm = pl.BlockSpec(memory_space=pl.ANY)
     dma = pltpu.SemaphoreType.DMA
     outs = pl.pallas_call(
         functools.partial(kernel, sizes),
         out_shape=(block, block, jax.ShapeDtypeStruct((n_params, 1, slab), jnp.float32), block),
         in_specs=[pl.BlockSpec(memory_space=pltpu.SMEM)]
-        + [pl.BlockSpec(memory_space=pl.ANY)] * 5
+        + [hbm] * 5
         + [vmem] * 4,
-        out_specs=(vmem,) * 4,
+        out_specs=(hbm, hbm, vmem, hbm),
         scratch_shapes=[
+            pltpu.VMEM((rows, slab), jnp.bfloat16),
+            pltpu.VMEM((rows, slab), jnp.bfloat16),
             pltpu.VMEM((rows, slab), jnp.bfloat16),
             pltpu.VMEM((rows, slab), jnp.bfloat16),
             pltpu.VMEM((rows, slab), jnp.bfloat16),
@@ -481,6 +508,7 @@
             pltpu.VMEM((n_seq, 8, slab), jnp.float32),
             dma((chunks,)),
             dma((4,)),
+            dma((2,)),
             dma((2, n_seq, chunks)),
             dma((2, n_seq, chunks)),
             dma((2, n_chan)),

time: 98.2 us -> 49.4 us (0.50)
  Pallas kernels: 97.4 us -> 48.6 us
    pallas_call x1, Pallas kernels: 50.5 us -> 2.27 us  [store(): pl.pallas_call(functools.partial(store_kernel, count), out_shape=tuple((j...]
where the time goes in v3:
time: 49.4 us; the launch traced here: 49.2 us
  Pallas kernels  48.6 us (98%)
  between operations  0.64 us (1%)
    pallas_call x1, Pallas kernels, per_device(): pl.pallas_call(functools.partial(kernel, sizes), out_shape=(block, block,...  46.3 us
    pallas_call x1, Pallas kernels, store(): pl.pallas_call(functools.partial(store_kernel, count), out_shape=tuple((j...  2.27 us

profile of v3, /device:TPU:0, one launch (start us, length us, event | category | flops | bytes accessed | tf_op | source)
XLA Modules:
  0.0 49.2 jit_solution(17817461882607699383)
XLA Ops:
  0.6 46.3 %shard_map.129 = (bf16[128,2048]{1,0:T(8,128)(2,1)}, bf16[128,2048]{1,0:T(8,128)(2,1)}, f32[7,1,2048]{2,1,0:T(1,128)}, bf16[128,2048]{1,0:T(8,128)(2,1)}) custom-call(s32[4]{0:T(128)} %order.1, bf16[128,2048]{1,0:T(8,128)(2,1)} %bitcast.11, bf16[128,2048]{1,0:T(8,128)(2,1)} %bitcast.12, bf16[128,2048]{1,0:T(8,128)(2,1)} %bitcast.13, ...), custom_call_target="tpu_custom_call" | custom-call | tf_op jit(solution)/shard_map/pallas_call | solution.py:484
  47.0 2.3 %shard_map.130 = (bf16[128,2048]{1,0:T(8,128)(2,1)}, bf16[128,2048]{1,0:T(8,128)(2,1)}, f32[7,1,2048]{2,1,0:T(1,128)}, bf16[128,2048]{1,0:T(8,128)(2,1)}) custom-call(bf16[128,2048]{1,0:T(8,128)(2,1)} %get-tuple-element.12.refs_0_, bf16[128,2048]{1,0:T(8,128)(2,1)} %get-tuple-element.13.refs_1_, f32[7,1,2048]{2,1,0:T(1,128)} %get-tuple-element.14.refs_2_, ...), custom_call_target="tpu_custom_call" | custom-call | tf_op jit(solution)/shard_map/pallas_call | solution.py:465

commit v4 on v3

--- a/solution.py
+++ b/solution.py
@@ -91,6 +91,8 @@
     sibling = chip * 2 + 1 - core
 
     def columns(c):
+        if isinstance(c, int):
+            return pl.ds(c * width, width)
         return pl.ds(pl.multiple_of(c * width, width), width)
 
     def same_core(j):
@@ -341,10 +343,13 @@
     cross_lanes[...] = jnp.zeros_like(cross_lanes)
     for c in range(early):
         relay(0, c)
-    lax.fori_loop(0, middle, backward_step, 0)
-    for c in range(early, chunks):
+    lax.fori_loop(0, chunks - 2, backward_step, 0)
+    for c in range(early, middle):
         start_own(0, c)
-    lax.fori_loop(middle, chunks, backward_step, 0)
+    backward_step(chunks - 2, 0)
+    for c in range(middle, chunks):
+        start_own(0, c)
+    backward_step(chunks - 1, 0)
 
     cross_rows[my_chan] = jnp.broadcast_to(
         jnp.sum(cross_lanes[...].T, axis=0, keepdims=True), (8, rows)

time: 49.4 us -> 49.4 us (level)
  no operation moved by 1% of the time
where the time goes in v4:
time: 49.4 us; the launch traced here: 49.2 us
  Pallas kernels  48.6 us (98%)
  between operations  0.64 us (1%)
    pallas_call x1, Pallas kernels, per_device(): pl.pallas_call(functools.partial(kernel, sizes), out_shape=(block, block,...  46.3 us
    pallas_call x1, Pallas kernels, store(): pl.pallas_call(functools.partial(store_kernel, count), out_shape=tuple((j...  2.27 us

profile of v4, /device:TPU:0, one launch (start us, length us, event | category | flops | bytes accessed | tf_op | source)
XLA Modules:
  0.0 49.2 jit_solution(1894971997676343156)
XLA Ops:
  0.6 46.3 %shard_map.129 = (bf16[128,2048]{1,0:T(8,128)(2,1)}, bf16[128,2048]{1,0:T(8,128)(2,1)}, f32[7,1,2048]{2,1,0:T(1,128)}, bf16[128,2048]{1,0:T(8,128)(2,1)}) custom-call(s32[4]{0:T(128)} %order.1, bf16[128,2048]{1,0:T(8,128)(2,1)} %bitcast.11, bf16[128,2048]{1,0:T(8,128)(2,1)} %bitcast.12, bf16[128,2048]{1,0:T(8,128)(2,1)} %bitcast.13, ...), custom_call_target="tpu_custom_call" | custom-call | tf_op jit(solution)/shard_map/pallas_call | solution.py:489
  46.9 2.3 %shard_map.130 = (bf16[128,2048]{1,0:T(8,128)(2,1)}, bf16[128,2048]{1,0:T(8,128)(2,1)}, f32[7,1,2048]{2,1,0:T(1,128)}, bf16[128,2048]{1,0:T(8,128)(2,1)}) custom-call(bf16[128,2048]{1,0:T(8,128)(2,1)} %get-tuple-element.12.refs_0_, bf16[128,2048]{1,0:T(8,128)(2,1)} %get-tuple-element.13.refs_1_, f32[7,1,2048]{2,1,0:T(1,128)} %get-tuple-element.14.refs_2_, ...), custom_call_target="tpu_custom_call" | custom-call | tf_op jit(solution)/shard_map/pallas_call | solution.py:470
